TPU v7x, 32 devices: a whole 2x2x4 slice. The times are simulated.
32 devices in a mesh: row: 8 (over z, y), col: 4 (over x, core).
Axes of the slice: x: 2, y: 2, z: 4, core: 2. Of those that a mesh axis runs over, the one named last changes fastest.
Arguments:
- orbitals: bfloat16 [32, 64000], P(('row', 'col')), may hold values from -6 to 6
- pair_list: int32 [32, 8, 2], P(('row', 'col')), may hold values from 0 to 7, as said below
- pair_count: int32 [32], P(('row', 'col')), may hold values from 1 to 8
Outputs:
- exchange_fields: float32 [32, 64000], P(('row', 'col'))
Inputs may be any that keep to these rules, and one draw needn't show every extreme that they name: pair_list[., ., 0] is below 4 and pair_list[., ., 1] below 8.
All inputs are finite; a program needn't handle non-finite values.
Results may differ from a plain program's by a relative error of at most 0.0004.
Values may be sent and summed in bfloat16 or wider, within the bound.
No kernel may reach another device: no remote copies, remote signals or barrier semaphores. Data moves between devices by JAX's collectives and lax.ppermute only.
A program may use at most 64 MiB of HBM per device.

v0:
```python
import functools
import itertools

import jax
import jax.numpy as jnp
import ml_dtypes
import numpy as np
from jax import lax
from jax.experimental import pallas as pl
from jax.experimental.pallas import tpu as pltpu
from jax.sharding import PartitionSpec as P

GX = 40
LANES = 128
SIDE = 3
THIRD = -(-GX // SIDE)
PACK = THIRD * GX
ROWS = SIDE * PACK
LIVE = GX * GX
SPARE = SIDE * GX
FLAT = LIVE * GX // LANES
CHUNK = PACK // 16
FLAT_ROWS = SIDE * CHUNK * 5 + 8
DUO = 2 * GX
QUAD = 4 * GX
GROUP = 10
VMEM_LIMIT = 20 * 1024 * 1024
screen_width = 0.9
F32 = jnp.float32
BF16 = jnp.bfloat16


def real_basis():
    half = GX // 2
    point = np.arange(GX)
    rows = [np.cos(2 * np.pi * (k * point % GX) / GX) for k in range(half + 1)]
    rows += [np.sin(2 * np.pi * (k * point % GX) / GX) for k in range(1, half)]
    frequency = np.concatenate([np.arange(half + 1), np.arange(1, half)])
    norm = np.where((frequency == 0) | (frequency == half), 1.0, 2.0) / GX
    return np.stack(rows), frequency, norm


def halves(table):
    high = table.astype(ml_dtypes.bfloat16)
    low = (table - high.astype(np.float64)).astype(ml_dtypes.bfloat16)
    return high, low


def left_table(table):
    high, low = halves(np.kron(np.eye(2), table))
    return np.concatenate([high, low, high], axis=1)


def right_table(table):
    wide = np.zeros((LANES, LANES))
    for p in range(SIDE):
        wide[p * GX : (p + 1) * GX, p * GX : (p + 1) * GX] = table
    high, low = halves(wide)
    both = np.concatenate([high, low], axis=1)
    return np.concatenate([both, both], axis=0)


def kernel_table():
    _, frequency, norm = real_basis()
    wave = frequency * (2.0 * np.pi / GX)
    squared = wave * wave
    total = squared[:, None, None] + squared[None, :, None] + squared[None, None, :]
    safe = np.where(total > 0, total, 1.0)
    screened = 4.0 * np.pi * (1.0 - np.exp(-safe / (4.0 * screen_width**2))) / safe
    kernel = np.where(total > 0, screened, np.pi / screen_width**2)
    kernel = kernel * norm[:, None, None] * norm[None, :, None] * norm[None, None, :]
    rows = np.swapaxes(kernel, 0, 1).reshape(LIVE, GX)
    out = np.zeros((LIVE, LANES), np.float32)
    for p in range(SIDE):
        out[:, p * GX : (p + 1) * GX] = rows
    return out


def place(out, row, col):
    for z in range(GX):
        out[row + z, col + z] = 1.0


def spread_table():
    out = np.zeros((SIDE * LANES, SIDE * LANES), np.float32)
    for third in range(SIDE):
        for p in range(SIDE):
            place(out, p * LANES + third * GX, third * LANES + p * GX)
    return out.astype(ml_dtypes.bfloat16)


def repeat_table():
    out = np.zeros((LANES, SIDE * LANES), np.float32)
    for third in range(SIDE):
        for p in range(SIDE):
            place(out, third * GX, third * LANES + p * GX)
    return out.astype(ml_dtypes.bfloat16)


def dot(a, b):
    return jnp.dot(a, b, preferred_element_type=F32)


def split(values):
    high = values.astype(BF16)
    return high, (values - high.astype(F32)).astype(BF16)


def contract_rows(table, values):
    high, low = split(values)
    return dot(table, jnp.concatenate([high, high, low], axis=0))


def contract_lanes(values, table):
    both = dot(jnp.concatenate(split(values), axis=1), table)
    return both[:, :LANES] + both[:, LANES:]


def fold(values):
    return jnp.concatenate([values[:DUO], values[DUO:]], axis=1)


def unfold(values):
    return jnp.concatenate([values[:, :LANES], values[:, LANES:]], axis=0)


def in_groups(body):
    def group(outer, carry):
        body([outer * GROUP + inner for inner in range(GROUP)])
        return carry

    lax.fori_loop(0, GX // 4 // GROUP, group, 0)


def quad(step):
    return pl.ds(step * QUAD, QUAD)


def load_planes(ref, step):
    planes = [ref[pl.ds(step * 4 + i, GX, stride=GX), :] for i in range(4)]
    left = jnp.concatenate(planes[:2], axis=0)
    return jnp.concatenate([left, jnp.concatenate(planes[2:], axis=0)], axis=1)


def store_planes(ref, step, values):
    for i in range(4):
        rows, lanes = i % 2 * GX, i // 2 * LANES
        ref[pl.ds(step * 4 + i, GX, stride=GX), :] = values[rows : rows + GX, lanes : lanes + LANES]


def count_vector(pairs, live):
    slots = pairs.shape[1]
    row = lax.broadcasted_iota(jnp.int32, (16, slots), 0)
    lane = lax.broadcasted_iota(jnp.int32, (LANES, slots), 0) - SPARE
    first = (pairs[0:1] == row) & (lax.broadcasted_iota(jnp.int32, (16, slots), 1) < live)
    second = jnp.where(pairs[1:2] == lane, 1.0, 0.0)
    contract = (((1,), (1,)), ((), ()))
    return lax.dot_general(jnp.where(first, 1.0, 0.0), second, contract, preferred_element_type=F32)


def unroll_rows(copy):
    for k in range(FLAT):
        copy(k, slice(k * LANES, (k + 1) * LANES))


def pack_kernel(band_ref, out_ref, flat_ref, wide_ref):
    def to_rows(k, lanes):
        flat_ref[k : k + 1, :] = band_ref[0:1, lanes].astype(F32)

    unroll_rows(to_rows)
    unused = FLAT_ROWS - FLAT
    flat_ref[FLAT:FLAT_ROWS, :] = jnp.zeros((unused, LANES), F32)
    lane = lax.broadcasted_iota(jnp.int32, (1, LANES), 1)
    for q in range(16):
        row, offset = divmod(q * GX, LANES)
        packed = jnp.zeros((CHUNK, LANES), F32)
        for third in range(SIDE):
            start = third * CHUNK * 5 + row
            values = flat_ref[pl.ds(start, CHUNK, stride=5), :]
            if offset + GX > LANES:
                after = flat_ref[pl.ds(start + 1, CHUNK, stride=5), :]
                values = jnp.where(lane >= offset, values, after)
            shift = (third * GX - offset) % LANES
            values = pltpu.roll(values, shift, 1) if shift else values
            packed = jnp.where(lane // GX == third, values, packed)
        wide_ref[pl.ds(q, CHUNK, stride=16), :] = packed
    out_ref[0] = wide_ref[...].astype(BF16)


def list_kernel(pairs_ref, live_ref, out_ref):
    out_ref[...] = count_vector(pairs_ref[0], live_ref[...])


def count_kernel(col_total, packed_ref, own_ref, mate_ref, out_ref):
    out_ref[...] = packed_ref[...]
    counts = own_ref[...] + pltpu.roll(mate_ref[...], col_total, 0)
    out_ref[0, 0:16, :] = (packed_ref[0, 0:16, :].astype(F32) + counts).astype(BF16)


def spread_waves(own_bands, repeat_ref, wave_refs):
    for band, wave_ref in zip(own_bands, wave_refs):
        wide = dot(band, repeat_ref[...])
        for third in range(SIDE):
            wave_ref[pl.ds(third * PACK, PACK), :] = wide[:, third * LANES : (third + 1) * LANES]


def clear(sum_refs):
    for sum_ref in sum_refs:
        sum_ref[...] = jnp.zeros_like(sum_ref)


def lane_side():
    return lax.broadcasted_iota(jnp.int32, (1, LANES), 1) // GX


def solve_trios(first, count, lists, load_band, tables, wave_refs, sum_refs, scratch):
    spread_ref, _, z_ref, z_back_ref, row_ref, row_back_ref, kernel_ref = tables
    trio_ref, partner_ref, work_ref, work2_ref = scratch
    slot_list, band_list, weight_list = lists
    side = lane_side()

    def by_side(values):
        row = jnp.zeros((1, LANES), F32)
        for p in range(SIDE):
            row = jnp.where(side == p, values[p].astype(F32), row)
        return row

    def trio(at, carry):
        places = [first + at * SIDE + p for p in range(SIDE)]
        for p, place in enumerate(places):
            load_band(slot_list[place], trio_ref, p)
        bands = [band_list[place] for place in places]
        weights = [weight_list[place] for place in places]
        is_mate = by_side(bands) > 0.5
        scales = [
            by_side([jnp.where(bands[p] == which, weights[p], 0) for p in range(SIDE)])
            for which in range(2)
        ]
        wide = dot(trio_ref[...], spread_ref[...])
        for third in range(SIDE):
            partner_ref[pl.ds(third * PACK, PACK), :] = wide[:, third * LANES : (third + 1) * LANES]

        def forward(steps):
            values = []
            for step in steps:
                wave = jnp.where(is_mate, wave_refs[1][quad(step), :], wave_refs[0][quad(step), :])
                values.append(partner_ref[quad(step), :] * wave)
            values = [contract_lanes(v, z_ref[...]) for v in values]
            values = [contract_rows(row_ref[...], fold(v)) for v in values]
            for step, v in zip(steps, values):
                work_ref[quad(step), :] = unfold(v)

        def across(steps):
            values = [load_planes(work_ref, step) for step in steps]
            values = [contract_rows(row_ref[...], v) for v in values]
            values = [v * fold(kernel_ref[quad(step), :]) for step, v in zip(steps, values)]
            values = [contract_rows(row_back_ref[...], v) for v in values]
            for step, v in zip(steps, values):
                store_planes(work2_ref, step, v)

        def back(steps):
            values = [fold(work2_ref[quad(step), :]) for step in steps]
            values = [unfold(contract_rows(row_back_ref[...], v)) for v in values]
            values = [contract_lanes(v, z_back_ref[...]) for v in values]
            for step, v in zip(steps, values):
                v = v * partner_ref[quad(step), :]
                for sum_ref, scale in zip(sum_refs, scales):
                    sum_ref[quad(step), :] = sum_ref[quad(step), :] + v * scale

        for phase in (forward, across, back):
            in_groups(phase)
        return carry

    lax.fori_loop(0, count, trio, 0)


def flat_fields(sum_refs, out_refs):
    lane = lax.broadcasted_iota(jnp.int32, (1, LANES), 1)
    rows = LIVE // 16
    for sum_ref, out_ref in zip(sum_refs, out_refs):
        flat = [jnp.zeros((rows, LANES), F32)] * 5
        for q in range(16):
            row, offset = divmod(q * GX, LANES)
            values = sum_ref[pl.ds(q, rows, stride=16), :]
            moved = jnp.zeros((rows, LANES), F32)
            for p in range(SIDE):
                shift = (offset - p * GX) % LANES
                moved = moved + (pltpu.roll(values, shift, 1) if shift else values)
            flat[row] = jnp.where(lane >= offset, moved, flat[row])
            if offset + GX > LANES:
                flat[row + 1] = jnp.where(lane < offset + GX - LANES, moved, flat[row + 1])
        for row in range(5):
            out_ref[pl.ds(row, rows, stride=5), :] = flat[row]


def near_kernel(row_total, col_total, part, *refs):
    stages = STAGES[: part + 1]
    blocks = [block for stage in stages for block in stage]
    band_refs, refs = refs[: len(blocks)], refs[len(blocks) :]
    bands = [(ref, at) for ref, block in zip(band_refs, blocks) for at in range(len(block))]
    flips = [flip for block in blocks for flip in block]
    mate_ref, tables, refs = refs[0], refs[1:8], refs[8:]
    if part:
        wave_refs, given_refs, out_refs, refs = refs[:2], refs[2:4], refs[4:6], refs[6:]
    else:
        wave_refs, out_refs, refs = refs[:2], refs[2:4], refs[4:]
    (count_vmem, count_smem, slot_list, band_list, weight_list), refs = refs[:5], refs[5:]
    scratch, sem = refs[:4], refs[4]
    sum_refs = refs[5:] if part == 2 else out_refs

    lane = lax.broadcasted_iota(jnp.int32, (8, LANES), 1)
    counts = jnp.zeros((8, LANES), F32)
    for s, (ref, at) in enumerate(bands):
        spare = ref[at, 0:16, :].astype(F32)[0:8]
        shift = (s * row_total - SPARE) % LANES
        moved = pltpu.roll(spare, shift, 1) if shift else spare
        counts = jnp.where(lane // row_total == s, moved, counts)
    count_vmem[...] = counts.astype(jnp.int32)
    copy = pltpu.make_async_copy(count_vmem, count_smem, sem)
    copy.start()
    if part:
        for sum_ref, given_ref in zip(sum_refs, given_refs):
            sum_ref[...] = given_ref[...]
    else:
        clear(sum_refs)
        spread_waves((band_refs[0][0], mate_ref[0]), tables[1], wave_refs)
    copy.wait()
    row = lax.axis_index("row")
    col = lax.axis_index("col")
    total = jnp.int32(0)
    done = jnp.int32(0)
    place = 0
    for step, stage in enumerate(stages):
        here = range(place, place + sum(len(block) for block in stage))
        place = here.stop
        for which, at in itertools.product(range(2), here):
            row_flip, col_flip = flips[at]
            row_place = flips.index((0, col_flip)) * row_total
            col_place = flips.index((row_flip, 0)) * row_total
            weight = count_smem[col ^ which, row_place + (row ^ row_flip)]
            if at or which:
                mirror = which * col_total + (col ^ col_flip)
                weight = weight + count_smem[mirror, col_place + row]
            slot_list[total] = at
            band_list[total] = which
            weight_list[total] = weight
            total = total + jnp.where(weight > 0, 1, 0)
        if step < 2:
            trios = jnp.minimum((total - done) // SIDE, CAPS[step])
            if step < part:
                done = done + trios * SIDE
    if part == 2:
        trios = (total - done + SIDE - 1) // SIDE
        for p in range(SIDE - 1):
            slot_list[total + p] = 0
            band_list[total + p] = 0
            weight_list[total + p] = 0

    def load_band(wanted, target, p):
        for place, (ref, at) in enumerate(bands):

            @pl.when(wanted == place)
            def _():
                target[:, p * LANES : (p + 1) * LANES] = ref[at]

    lists = (slot_list, band_list, weight_list)
    solve_trios(done, trios, lists, load_band, tables, wave_refs, sum_refs, scratch)
    if part == 2:
        flat_fields(sum_refs, out_refs)


def far_kernel(total_ref, slot_list, band_list, weight_list, bands_ref, own_ref, mate_ref, *refs):
    tables, out_refs, refs = refs[:7], refs[7:9], refs[9:]
    buffer, wave_refs, sum_refs, scratch = refs[0], refs[1:3], refs[3:5], refs[5:]
    spread_waves((own_ref[0], mate_ref[0]), tables[1], wave_refs)
    clear(sum_refs)

    def load_band(place, target, p):
        pltpu.sync_copy(bands_ref.at[place], buffer)
        target[:, p * LANES : (p + 1) * LANES] = buffer[...]

    lists = (slot_list, band_list, weight_list)
    trios = (total_ref[0] + SIDE - 1) // SIDE
    solve_trios(0, trios, lists, load_band, tables, wave_refs, sum_refs, scratch)
    flat_fields(sum_refs, out_refs)


def finish_kernel(own_ref, part_ref, out_ref):
    def to_lanes(k, lanes):
        out_ref[0:1, lanes] = own_ref[k : k + 1, :] + part_ref[k : k + 1, :]

    unroll_rows(to_lanes)


VMEM_SPEC = pl.BlockSpec(memory_space=pltpu.VMEM)
SMEM_SPEC = pl.BlockSpec(memory_space=pltpu.SMEM)
ANY_SPEC = pl.BlockSpec(memory_space=pl.ANY)
PARAMS = pltpu.CompilerParams(vmem_limit_bytes=VMEM_LIMIT)


def solve_tables():
    basis, _, _ = real_basis()
    return [
        spread_table(),
        repeat_table(),
        right_table(basis.T),
        right_table(basis),
        left_table(basis),
        left_table(basis.T),
        kernel_table(),
    ]


def solve_scratch():
    return [pltpu.VMEM((PACK, SIDE * LANES), BF16)] + [pltpu.VMEM((ROWS, LANES), F32)] * 3


def pair_of(rows):
    return [jax.ShapeDtypeStruct((rows, LANES), F32)] * 2


def swap(values, axis, size, flip):
    return lax.ppermute(values, axis, [(i, i ^ flip) for i in range(size)])


def count_pairs(pair_list, pair_count, row_total, col_total):
    slots = pair_list.shape[1]
    live = lax.iota(jnp.int32, slots) < pair_count[0]
    first = pair_list[0, :, 0][:, None, None] == lax.iota(jnp.int32, col_total)[None, :, None]
    second = pair_list[0, :, 1][:, None, None] == lax.iota(jnp.int32, row_total)[None, None, :]
    return jnp.sum((first & second & live[:, None, None]).astype(F32), axis=0)


def pack_band(orbitals):
    return pl.pallas_call(
        pack_kernel,
        out_shape=jax.ShapeDtypeStruct((1, PACK, LANES), BF16),
        in_specs=[VMEM_SPEC],
        out_specs=VMEM_SPEC,
        scratch_shapes=[pltpu.VMEM((FLAT_ROWS, LANES), F32), pltpu.VMEM((PACK, LANES), F32)],
        compiler_params=PARAMS,
        name="pack_band",
    )(orbitals)


def list_counts(pair_list, pair_count):
    return pl.pallas_call(
        list_kernel,
        out_shape=jax.ShapeDtypeStruct((16, LANES), F32),
        in_specs=[VMEM_SPEC] * 2,
        out_specs=VMEM_SPEC,
        compiler_params=PARAMS,
        name="list_counts",
    )(jnp.swapaxes(pair_list, 1, 2), pair_count.reshape(1, 1))


def add_counts(packed, col_total, counts, mate_counts):
    return pl.pallas_call(
        functools.partial(count_kernel, col_total),
        out_shape=jax.ShapeDtypeStruct(packed.shape, BF16),
        in_specs=[VMEM_SPEC] * 3,
        out_specs=VMEM_SPEC,
        compiler_params=PARAMS,
        name="add_counts",
    )(packed, counts, mate_counts)


def finish(own, part):
    return pl.pallas_call(
        finish_kernel,
        out_shape=jax.ShapeDtypeStruct((1, LIVE * GX), F32),
        in_specs=[VMEM_SPEC] * 2,
        out_specs=VMEM_SPEC,
        compiler_params=PARAMS,
        name="add_parts",
    )(own, part)


NEAR = (8, 4)
STAGES = (
    (((0, 0),), ((4, 0),), ((2, 0),), ((1, 0),), ((0, 2),), ((1, 2),)),
    (((4, 2), (2, 2)), ((5, 0), (3, 0)), ((6, 0), (3, 2))),
    (((5, 2),), ((6, 2), (7, 0)), ((7, 2),)),
)
CAPS = (2, 2)


def near_part(row_total, col_total, part, operands):
    places = 2 * row_total * (col_total // 2) + SIDE
    out_shape = pair_of(ROWS)
    if part == 0:
        out_shape = out_shape * 2
    if part == 2:
        out_shape = pair_of(FLAT)
    operands = list(operands)
    cost = pl.CostEstimate(flops=4 * 10**9, bytes_accessed=2 * 10**7, transcendentals=0)
    return pl.pallas_call(
        functools.partial(near_kernel, row_total, col_total, part),
        out_shape=out_shape,
        in_specs=[VMEM_SPEC] * len(operands),
        out_specs=[VMEM_SPEC] * len(out_shape),
        scratch_shapes=[
            pltpu.VMEM((8, LANES), jnp.int32),
            pltpu.SMEM((8, LANES), jnp.int32),
            pltpu.SMEM((places,), jnp.int32),
            pltpu.SMEM((places,), jnp.int32),
            pltpu.SMEM((places,), jnp.int32),
        ]
        + solve_scratch()
        + [pltpu.SemaphoreType.DMA]
        + [pltpu.VMEM((ROWS, LANES), F32)] * (2 if part == 2 else 0),
        compiler_params=PARAMS,
        cost_estimate=cost,
        name="solve_part",
    )(*operands)


def near_shards(row_total, col_total, orbitals, pair_list, pair_count):
    row_swap = lambda values, flip: swap(values, "row", row_total, flip)
    col_swap = lambda values, flip: swap(values, "col", col_total, flip)
    both = lambda a, b: jnp.concatenate([a, b], axis=0)

    def corner_swap(values):
        places = list(itertools.product(range(row_total), range(col_total)))
        at = lambda row, col: row * col_total + col
        pairs = [(at(row, col), at(row ^ 1, col ^ 2)) for row, col in places]
        return lax.ppermute(values, ("row", "col"), pairs)

    counts = list_counts(pair_list, pair_count)
    own = add_counts(pack_band(orbitals), col_total, counts, col_swap(counts, 1))
    mate, x, y, z = col_swap(own, 1), col_swap(own, 2), row_swap(own, 1), row_swap(own, 2)
    xy, w = corner_swap(own), row_swap(own, 4)
    mate, x, y, z, xy, w = lax.optimization_barrier((mate, x, y, z, xy, w))
    over_x, over_y, over_z = (
        col_swap(both(w, z), 2),
        row_swap(both(w, z), 1),
        row_swap(both(w, xy), 2),
    )
    tables = [jnp.asarray(table) for table in solve_tables()]
    blocks = [own, w, z, y, x, xy]
    *waves, sum0, sum1 = near_part(row_total, col_total, 0, [*blocks, mate, *tables])
    held = lax.optimization_barrier((sum0, sum1, over_x, over_y, over_z))
    sum0, sum1, over_x, over_y, over_z = held
    last = (
        row_swap(over_x[:1], 1),
        row_swap(both(over_x[:1], over_y[:1]), 2),
        corner_swap(over_z[:1]),
    )
    for part, arrived in enumerate(((over_x, over_y, over_z), last), 1):
        blocks += arrived
        operands = [*blocks, mate, *tables, *waves, sum0, sum1]
        sum0, sum1 = near_part(row_total, col_total, part, operands)
    return finish(sum0, col_swap(sum1, 1))


def far_shards(row_total, col_total, orbitals, pair_list, pair_count):
    counts = count_pairs(pair_list, pair_count, row_total, col_total)
    own = pack_band(orbitals)
    axes = ("row", "col")
    table = lax.all_gather(counts.reshape(-1), axes)
    table = table.reshape(row_total, col_total, col_total, row_total)
    wide = col_total // 2
    column = lax.all_gather(own[0], "row")
    columns = [column] + [swap(column, "col", col_total, 2 * x) for x in range(1, wide)]
    bands = jnp.concatenate(columns, axis=0)
    row = lax.axis_index("row")
    col = lax.axis_index("col")
    mine = jnp.stack([col, col ^ 1])
    other_col = ((col // 2) ^ lax.iota(jnp.int32, wide)) * 2 + col % 2
    other_row = lax.iota(jnp.int32, row_total)
    direct = table[row][other_col][:, mine]
    direct = jnp.transpose(direct, (1, 2, 0))
    mirror = table[:, :, :, row][:, mine][:, :, other_col]
    mirror = jnp.transpose(mirror, (1, 0, 2))
    same = (mine[:, None, None] == other_col[None, None, :]) & (other_row == row)[None, :, None]
    weights = (direct + jnp.where(same, 0.0, mirror)).astype(jnp.int32).reshape(-1)
    index = lax.iota(jnp.int32, weights.shape[0])
    order = jnp.argsort(jnp.where(weights > 0, 0, 1), stable=True)
    pad = lambda values: jnp.pad(values.astype(jnp.int32), (0, SIDE))
    slots = row_total * wide
    slot = order % slots
    band = (slot % wide) * row_total + slot // wide
    total = jnp.sum((weights > 0).astype(jnp.int32)).reshape(1)
    fields = pl.pallas_call(
        far_kernel,
        out_shape=pair_of(FLAT),
        in_specs=[SMEM_SPEC] * 4 + [ANY_SPEC] + [VMEM_SPEC] * 9,
        out_specs=[VMEM_SPEC] * 2,
        scratch_shapes=[pltpu.VMEM((PACK, LANES), BF16)]
        + [pltpu.VMEM((ROWS, LANES), F32)] * 4
        + solve_scratch(),
        compiler_params=PARAMS,
        name="solve_pairs",
    )(
        total,
        pad(band),
        pad(order // slots),
        pad(weights[order]),
        bands,
        own,
        swap(own, "col", col_total, 1),
        *map(jnp.asarray, solve_tables()),
    )
    return finish(fields[0], swap(fields[1], "col", col_total, 1))


def solution(mesh):
    row_total, col_total = mesh.shape["row"], mesh.shape["col"]
    near = (row_total, col_total) == NEAR
    shards = near_shards if near else far_shards
    return jax.shard_map(
        functools.partial(shards, row_total, col_total),
        mesh=mesh,
        in_specs=(P(("row", "col"), None), P(("row", "col"), None, None), P(("row", "col"))),
        out_specs=P(("row", "col"), None),
        check_vma=False,
    )
```

profile of v0, /device:TPU:0, one launch (start us, length us, event | category | flops | bytes accessed | tf_op | source)
XLA Modules:
  0.0 47.0 jit_solution(12587664306277801334)
XLA Ops:
  0.7 0.7 %copy-done.1 = s32[1,8,2]{1,2,0:T(2,128)S(1)} copy-done((s32[1,8,2]{1,2,0:T(2,128)S(1)}, s32[1,8,2]{1,2,0:T(2,128)}, u32[]{:S(2)}) %copy-start.1) | copy-done | bytes 88
  1.3 0.2 list_counts.1.own_ref
  1.5 0.5 %collective-permute-start = (f32[16,128]{1,0:T(8,128)S(1)}, f32[16,128]{1,0:T(8,128)S(1)}, u32[]{:S(2)}, u32[]{:S(2)}) collective-permute-start(f32[16,128]{1,0:T(8,128)S(1)} %list_counts.1.own_ref), channel_id=1, source_target_pairs={{0,1},{1,0},{2,3},{3,2},{4,5},{5,4},{6,7},{7,6},{8,9},{9,8},{10,11... | collective-permute-start | bytes 24584 | tf_op jit(solution)/shard_map/ppermute | solution.py:423
  2.0 0.9 %copy-done = bf16[1,64000]{1,0:T(2,128)(2,1)S(1)} copy-done((bf16[1,64000]{1,0:T(2,128)(2,1)S(1)}, bf16[1,64000]{1,0:T(2,128)(2,1)}, u32[]{:S(2)}) %copy-start) | copy-done | bytes 128024
  2.9 0.4 pack_band.1.packed_ref
  3.3 0.0 copy-start.2
  3.3 3.7 %collective-permute-start.6 = (bf16[1,560,128]{2,1,0:T(8,128)(2,1)S(1)}, bf16[1,560,128]{2,1,0:T(8,128)(2,1)S(1)}, u32[]{:S(2)}, u32[]{:S(2)}) collective-permute-start(bf16[1,560,128]{2,1,0:T(8,128)(2,1)S(1)} %add_counts.1.refs_0_), channel_id=1, source_target_pairs={{0,16},{4,20},{8,24},{12,28},{16,0},{20,4},{24,8},{28,12},{1,17},{... | collective-permute-start | bytes 430088 | tf_op jit(solution)/shard_map/ppermute | solution.py:423
  7.0 2.4 %collective-permute-start.5 = (bf16[1,560,128]{2,1,0:T(8,128)(2,1)S(1)}, bf16[1,560,128]{2,1,0:T(8,128)(2,1)S(1)}, u32[]{:S(2)}, u32[]{:S(2)}) collective-permute-start(bf16[1,560,128]{2,1,0:T(8,128)(2,1)S(1)} %add_counts.1.refs_0_), channel_id=1, source_target_pairs={{0,6},{1,7},{2,4},{3,5},{4,2},{5,3},{6,0},{7,1},{8,14},{9,15},{10,... | collective-permute-start | bytes 430088 | tf_op jit(solution)/shard_map/ppermute | solution.py:527
  9.4 1.6 %collective-permute-start.4 = (bf16[1,560,128]{2,1,0:T(8,128)(2,1)S(1)}, bf16[1,560,128]{2,1,0:T(8,128)(2,1)S(1)}, u32[]{:S(2)}, u32[]{:S(2)}) collective-permute-start(bf16[1,560,128]{2,1,0:T(8,128)(2,1)S(1)} %add_counts.1.refs_0_), channel_id=1, source_target_pairs={{0,8},{4,12},{8,0},{12,4},{16,24},{20,28},{24,16},{28,20},{1,9},{5... | collective-permute-start | bytes 430088 | tf_op jit(solution)/shard_map/ppermute | solution.py:423
  11.0 0.5 %collective-permute-start.3 = (bf16[1,560,128]{2,1,0:T(8,128)(2,1)S(1)}, bf16[1,560,128]{2,1,0:T(8,128)(2,1)S(1)}, u32[]{:S(2)}, u32[]{:S(2)}) collective-permute-start(bf16[1,560,128]{2,1,0:T(8,128)(2,1)S(1)} %add_counts.1.refs_0_), channel_id=1, source_target_pairs={{0,4},{4,0},{8,12},{12,8},{16,20},{20,16},{24,28},{28,24},{1,5},{5... | collective-permute-start | bytes 430088 | tf_op jit(solution)/shard_map/ppermute | solution.py:423
  11.5 0.5 %collective-permute-start.2 = (bf16[1,560,128]{2,1,0:T(8,128)(2,1)S(1)}, bf16[1,560,128]{2,1,0:T(8,128)(2,1)S(1)}, u32[]{:S(2)}, u32[]{:S(2)}) collective-permute-start(bf16[1,560,128]{2,1,0:T(8,128)(2,1)S(1)} %add_counts.1.refs_0_), channel_id=1, source_target_pairs={{0,2},{1,3},{2,0},{3,1},{4,6},{5,7},{6,4},{7,5},{8,10},{9,11},{10,... | collective-permute-start | bytes 430088 | tf_op jit(solution)/shard_map/ppermute | solution.py:423
  12.1 2.5 %collective-permute-done.6.refs_1_ = bf16[1,560,128]{2,1,0:T(8,128)(2,1)S(1)} collective-permute-done((bf16[1,560,128]{2,1,0:T(8,128)(2,1)S(1)}, bf16[1,560,128]{2,1,0:T(8,128)(2,1)S(1)}, u32[]{:S(2)}, u32[]{:S(2)}) %collective-permute-start.6) | collective-permute-done | bytes 143392 | tf_op jit(solution)/shard_map/ppermute | solution.py:423
  14.6 2.4 %collective-permute-done.4.refs_2_ = bf16[1,560,128]{2,1,0:T(8,128)(2,1)S(1)} collective-permute-done((bf16[1,560,128]{2,1,0:T(8,128)(2,1)S(1)}, bf16[1,560,128]{2,1,0:T(8,128)(2,1)S(1)}, u32[]{:S(2)}, u32[]{:S(2)}) %collective-permute-start.4) | collective-permute-done | bytes 143392 | tf_op jit(solution)/shard_map/ppermute | solution.py:423
  17.0 0.0 copy-start.7
  17.0 0.0 copy-start.3
  17.1 1.5 %collective-permute-start.8 = (bf16[2,560,128]{2,1,0:T(8,128)(2,1)S(1)}, bf16[2,560,128]{2,1,0:T(8,128)(2,1)S(1)}, u32[]{:S(2)}, u32[]{:S(2)}) collective-permute-start(bf16[2,560,128]{2,1,0:T(8,128)(2,1)S(1)} %constant_dynamic-update-slice_fusion), channel_id=1, source_target_pairs={{0,4},{4,0},{8,12},{12,8},{16,20},{20,16},{24,28},{28,24},{1,5},{5... | collective-permute-start | bytes 860168 | tf_op jit(solution)/shard_map/ppermute | solution.py:423
  18.5 1.5 %collective-permute-start.7 = (bf16[2,560,128]{2,1,0:T(8,128)(2,1)S(1)}, bf16[2,560,128]{2,1,0:T(8,128)(2,1)S(1)}, u32[]{:S(2)}, u32[]{:S(2)}) collective-permute-start(bf16[2,560,128]{2,1,0:T(8,128)(2,1)S(1)} %constant_dynamic-update-slice_fusion), channel_id=1, source_target_pairs={{0,2},{1,3},{2,0},{3,1},{4,6},{5,7},{6,4},{7,5},{8,10},{9,11},{10,... | collective-permute-start | bytes 860168 | tf_op jit(solution)/shard_map/ppermute | solution.py:423
  20.1 1.1 %collective-permute-start.9 = (bf16[2,560,128]{2,1,0:T(8,128)(2,1)S(1)}, bf16[2,560,128]{2,1,0:T(8,128)(2,1)S(1)}, u32[]{:S(2)}, u32[]{:S(2)}) collective-permute-start(bf16[2,560,128]{2,1,0:T(8,128)(2,1)S(1)} %pad_maximum_fusion), channel_id=1, source_target_pairs={{0,8},{4,12},{8,0},{12,4},{16,24},{20,28},{24,16},{28,20},{1,9},{5... | collective-permute-start | bytes 860168 | tf_op jit(solution)/shard_map/ppermute | solution.py:423
  21.2 3.4 %solve_part.3 = (f32[1680,128]{1,0:T(8,128)S(1)}, f32[1680,128]{1,0:T(8,128)S(1)}, f32[1680,128]{1,0:T(8,128)S(1)}, f32[1680,128]{1,0:T(8,128)S(1)}) custom-call(bf16[1,560,128]{2,1,0:T(8,128)(2,1)S(1)} %add_counts.1.refs_0_, bf16[1,560,128]{2,1,0:T(8,128)(2,1)S(1)} %collective-permute-done.6.refs_1_, ...), custom_call_target="tpu_custom_call" | custom-call | flops 4000000000 | bytes 20000000 | tf_op jit(solution)/shard_map/solve_part/pallas_call | solution.py:497
  24.7 0.9 %collective-permute-done.8.refs_7_ = bf16[2,560,128]{2,1,0:T(8,128)(2,1)S(1)} collective-permute-done((bf16[2,560,128]{2,1,0:T(8,128)(2,1)S(1)}, bf16[2,560,128]{2,1,0:T(8,128)(2,1)S(1)}, u32[]{:S(2)}, u32[]{:S(2)}) %collective-permute-start.8) | collective-permute-done | bytes 286752 | tf_op jit(solution)/shard_map/ppermute | solution.py:423
  25.6 1.5 %collective-permute-done.7.refs_6_ = bf16[2,560,128]{2,1,0:T(8,128)(2,1)S(1)} collective-permute-done((bf16[2,560,128]{2,1,0:T(8,128)(2,1)S(1)}, bf16[2,560,128]{2,1,0:T(8,128)(2,1)S(1)}, u32[]{:S(2)}, u32[]{:S(2)}) %collective-permute-start.7) | collective-permute-done | bytes 286752 | tf_op jit(solution)/shard_map/ppermute | solution.py:423
  27.0 1.3 %collective-permute-done.9.refs_8_ = bf16[2,560,128]{2,1,0:T(8,128)(2,1)S(1)} collective-permute-done((bf16[2,560,128]{2,1,0:T(8,128)(2,1)S(1)}, bf16[2,560,128]{2,1,0:T(8,128)(2,1)S(1)}, u32[]{:S(2)}, u32[]{:S(2)}) %collective-permute-start.9) | collective-permute-done | bytes 286752 | tf_op jit(solution)/shard_map/ppermute | solution.py:423
  28.4 0.6 %collective-permute-start.10 = (bf16[1,560,128]{2,1,0:T(8,128)(2,1)S(1)}, bf16[1,560,128]{2,1,0:T(8,128)(2,1)S(1)}, u32[]{:S(2)}, u32[]{:S(2)}) collective-permute-start(bf16[1,560,128]{2,1,0:T(8,128)(2,1)S(1)} %slice.10), channel_id=1, source_target_pairs={{0,4},{4,0},{8,12},{12,8},{16,20},{20,16},{24,28},{28,24},{1,5},{5... | collective-permute-start | bytes 430088 | tf_op jit(solution)/shard_map/ppermute | solution.py:423
  29.0 1.6 %collective-permute-start.12 = (bf16[1,560,128]{2,1,0:T(8,128)(2,1)S(1)}, bf16[1,560,128]{2,1,0:T(8,128)(2,1)S(1)}, u32[]{:S(2)}, u32[]{:S(2)}) collective-permute-start(bf16[1,560,128]{2,1,0:T(8,128)(2,1)S(1)} %slice.12), channel_id=1, source_target_pairs={{0,6},{1,7},{2,4},{3,5},{4,2},{5,3},{6,0},{7,1},{8,14},{9,15},{10,... | collective-permute-start | bytes 430088 | tf_op jit(solution)/shard_map/ppermute | solution.py:527
  30.5 1.6 %collective-permute-start.11 = (bf16[2,560,128]{2,1,0:T(8,128)(2,1)S(1)}, bf16[2,560,128]{2,1,0:T(8,128)(2,1)S(1)}, u32[]{:S(2)}, u32[]{:S(2)}) collective-permute-start(bf16[2,560,128]{2,1,0:T(8,128)(2,1)S(1)} %pad_maximum_fusion.1), channel_id=1, source_target_pairs={{0,8},{4,12},{8,0},{12,4},{16,24},{20,28},{24,16},{28,20},{1,9},{5... | collective-permute-start | bytes 860168 | tf_op jit(solution)/shard_map/ppermute | solution.py:423
  32.1 3.3 %solve_part.4 = (f32[1680,128]{1,0:T(8,128)S(1)}, f32[1680,128]{1,0:T(8,128)S(1)}) custom-call(bf16[1,560,128]{2,1,0:T(8,128)(2,1)S(1)} %add_counts.1.refs_0_, bf16[1,560,128]{2,1,0:T(8,128)(2,1)S(1)} %collective-permute-done.6.refs_1_, bf16[1,560,128]{2,1,0:T(8,128)(2,1)S(1)} %collective-permute-done.4.refs_2_, ...), custom_call_target="tpu_custom_call" | custom-call | flops 4000000000 | bytes 20000000 | tf_op jit(solution)/shard_map/solve_part/pallas_call | solution.py:497
  35.5 0.2 collective-permute-done.10.refs_9_
  35.7 1.6 %collective-permute-done.11.refs_10_ = bf16[2,560,128]{2,1,0:T(8,128)(2,1)S(1)} collective-permute-done((bf16[2,560,128]{2,1,0:T(8,128)(2,1)S(1)}, bf16[2,560,128]{2,1,0:T(8,128)(2,1)S(1)}, u32[]{:S(2)}, u32[]{:S(2)}) %collective-permute-start.11) | collective-permute-done | bytes 286752 | tf_op jit(solution)/shard_map/ppermute | solution.py:423
  37.3 7.2 %solve_part.5 = (f32[500,128]{1,0:T(8,128)S(1)}, f32[500,128]{1,0:T(8,128)S(1)}) custom-call(bf16[1,560,128]{2,1,0:T(8,128)(2,1)S(1)} %add_counts.1.refs_0_, bf16[1,560,128]{2,1,0:T(8,128)(2,1)S(1)} %collective-permute-done.6.refs_1_, bf16[1,560,128]{2,1,0:T(8,128)(2,1)S(1)} %collective-permute-done.4.refs_2_, ...), custom_call_target="tpu_custom_call" | custom-call | flops 4000000000 | bytes 20000000 | tf_op jit(solution)/shard_map/solve_part/pallas_call | solution.py:497
  44.5 0.1 collective-permute-start.13
  44.5 1.5 %collective-permute-done.13.part_ref = f32[500,128]{1,0:T(8,128)S(1)} collective-permute-done((f32[500,128]{1,0:T(8,128)S(1)}, f32[500,128]{1,0:T(8,128)S(1)}, u32[]{:S(2)}, u32[]{:S(2)}) %collective-permute-start.13) | collective-permute-done | bytes 256032 | tf_op jit(solution)/shard_map/ppermute | solution.py:423
  46.1 1.0 %add_parts.1 = f32[1,64000]{1,0:T(1,128)} custom-call(f32[500,128]{1,0:T(8,128)S(1)} %get-tuple-element.41.own_ref, f32[500,128]{1,0:T(8,128)S(1)} %collective-permute-done.13.part_ref), custom_call_target="tpu_custom_call" | custom-call | tf_op jit(solution)/shard_map/add_parts/pallas_call | solution.py:469
  (28 shorter events, 0.2 us)
Async XLA Ops:
  0.7 0.7 %copy-start.1 = (s32[1,8,2]{1,2,0:T(2,128)S(1)}, s32[1,8,2]{1,2,0:T(2,128)}, u32[]{:S(2)}) copy-start(s32[1,8,2]{1,2,0:T(2,128)} %param.11) | copy-start | bytes 196
  1.5 1.8 %collective-permute-start = (f32[16,128]{1,0:T(8,128)S(1)}, f32[16,128]{1,0:T(8,128)S(1)}, u32[]{:S(2)}, u32[]{:S(2)}) collective-permute-start(f32[16,128]{1,0:T(8,128)S(1)} %list_counts.1.own_ref), channel_id=1, source_target_pairs={{0,1},{1,0},{2,3},{3,2},{4,5},{5,4},{6,7},{7,6},{8,9},{9,8},{10,11... | collective-permute-start | bytes 24584 | tf_op jit(solution)/shard_map/ppermute | solution.py:423
  2.0 0.9 %copy-start = (bf16[1,64000]{1,0:T(2,128)(2,1)S(1)}, bf16[1,64000]{1,0:T(2,128)(2,1)}, u32[]{:S(2)}) copy-start(bf16[1,64000]{1,0:T(2,128)(2,1)} %band_ref.1) | copy-start | bytes 384004
  2.9 18.3 %copy-start.6 = (bf16[128,384]{1,0:T(8,128)(2,1)S(1)}, bf16[128,384]{1,0:T(8,128)(2,1)}, u32[]{:S(2)}) copy-start(bf16[128,384]{1,0:T(8,128)(2,1)} %constant.15.clone.refs_8_.refs_11_.refs_14_) | copy-start | bytes 294916
  2.9 18.3 %copy-start.8 = (bf16[80,240]{1,0:T(8,128)(2,1)S(1)}, bf16[80,240]{1,0:T(8,128)(2,1)}, u32[]{:S(2)}) copy-start(bf16[80,240]{1,0:T(8,128)(2,1)} %constant.18.clone.refs_11_.refs_14_.refs_17_) | copy-start | bytes 115204
  3.3 17.9 %copy-start.2 = (f32[1600,128]{1,0:T(8,128)S(1)}, f32[1600,128]{1,0:T(8,128)}, u32[]{:S(2)}) copy-start(f32[1600,128]{1,0:T(8,128)} %constant.20.clone.refs_13_.refs_16_.refs_19_) | copy-start | bytes 2457604
  3.3 11.3 %collective-permute-start.6 = (bf16[1,560,128]{2,1,0:T(8,128)(2,1)S(1)}, bf16[1,560,128]{2,1,0:T(8,128)(2,1)S(1)}, u32[]{:S(2)}, u32[]{:S(2)}) collective-permute-start(bf16[1,560,128]{2,1,0:T(8,128)(2,1)S(1)} %add_counts.1.refs_0_), channel_id=1, source_target_pairs={{0,16},{4,20},{8,24},{12,28},{16,0},{20,4},{24,8},{28,12},{1,17},{... | collective-permute-start | bytes 430088 | tf_op jit(solution)/shard_map/ppermute | solution.py:423
  7.0 7.6 %collective-permute-start.5 = (bf16[1,560,128]{2,1,0:T(8,128)(2,1)S(1)}, bf16[1,560,128]{2,1,0:T(8,128)(2,1)S(1)}, u32[]{:S(2)}, u32[]{:S(2)}) collective-permute-start(bf16[1,560,128]{2,1,0:T(8,128)(2,1)S(1)} %add_counts.1.refs_0_), channel_id=1, source_target_pairs={{0,6},{1,7},{2,4},{3,5},{4,2},{5,3},{6,0},{7,1},{8,14},{9,15},{10,... | collective-permute-start | bytes 430088 | tf_op jit(solution)/shard_map/ppermute | solution.py:527
  9.4 7.5 %collective-permute-start.4 = (bf16[1,560,128]{2,1,0:T(8,128)(2,1)S(1)}, bf16[1,560,128]{2,1,0:T(8,128)(2,1)S(1)}, u32[]{:S(2)}, u32[]{:S(2)}) collective-permute-start(bf16[1,560,128]{2,1,0:T(8,128)(2,1)S(1)} %add_counts.1.refs_0_), channel_id=1, source_target_pairs={{0,8},{4,12},{8,0},{12,4},{16,24},{20,28},{24,16},{28,20},{1,9},{5... | collective-permute-start | bytes 430088 | tf_op jit(solution)/shard_map/ppermute | solution.py:423
  11.0 5.9 %collective-permute-start.3 = (bf16[1,560,128]{2,1,0:T(8,128)(2,1)S(1)}, bf16[1,560,128]{2,1,0:T(8,128)(2,1)S(1)}, u32[]{:S(2)}, u32[]{:S(2)}) collective-permute-start(bf16[1,560,128]{2,1,0:T(8,128)(2,1)S(1)} %add_counts.1.refs_0_), channel_id=1, source_target_pairs={{0,4},{4,0},{8,12},{12,8},{16,20},{20,16},{24,28},{28,24},{1,5},{5... | collective-permute-start | bytes 430088 | tf_op jit(solution)/shard_map/ppermute | solution.py:423
  11.5 5.4 %collective-permute-start.2 = (bf16[1,560,128]{2,1,0:T(8,128)(2,1)S(1)}, bf16[1,560,128]{2,1,0:T(8,128)(2,1)S(1)}, u32[]{:S(2)}, u32[]{:S(2)}) collective-permute-start(bf16[1,560,128]{2,1,0:T(8,128)(2,1)S(1)} %add_counts.1.refs_0_), channel_id=1, source_target_pairs={{0,2},{1,3},{2,0},{3,1},{4,6},{5,7},{6,4},{7,5},{8,10},{9,11},{10,... | collective-permute-start | bytes 430088 | tf_op jit(solution)/shard_map/ppermute | solution.py:423
  14.6 2.4 %collective-permute-start.1 = (bf16[1,560,128]{2,1,0:T(8,128)(2,1)S(1)}, bf16[1,560,128]{2,1,0:T(8,128)(2,1)S(1)}, u32[]{:S(2)}, u32[]{:S(2)}) collective-permute-start(bf16[1,560,128]{2,1,0:T(8,128)(2,1)S(1)} %add_counts.1.refs_0_), channel_id=1, source_target_pairs={{0,1},{1,0},{2,3},{3,2},{4,5},{5,4},{6,7},{7,6},{8,9},{9,8},{10,11... | collective-permute-start | bytes 430088 | tf_op jit(solution)/shard_map/ppermute | solution.py:423
  17.0 4.2 %copy-start.7 = (bf16[80,240]{1,0:T(8,128)(2,1)S(1)}, bf16[80,240]{1,0:T(8,128)(2,1)}, u32[]{:S(2)}) copy-start(bf16[80,240]{1,0:T(8,128)(2,1)} %constant.19.clone.refs_12_.refs_15_.refs_18_) | copy-start | bytes 115204
  17.0 4.2 %copy-start.3 = (bf16[384,384]{1,0:T(8,128)(2,1)S(1)}, bf16[384,384]{1,0:T(8,128)(2,1)}, u32[]{:S(2)}) copy-start(bf16[384,384]{1,0:T(8,128)(2,1)} %constant.14.clone.refs_7_.refs_10_.refs_13_) | copy-start | bytes 884740
  17.0 4.2 %copy-start.4 = (bf16[256,256]{1,0:T(8,128)(2,1)S(1)}, bf16[256,256]{1,0:T(8,128)(2,1)}, u32[]{:S(2)}) copy-start(bf16[256,256]{1,0:T(8,128)(2,1)} %constant.17.clone.refs_10_.refs_13_.refs_16_) | copy-start | bytes 393220
  17.1 4.2 %copy-start.5 = (bf16[256,256]{1,0:T(8,128)(2,1)S(1)}, bf16[256,256]{1,0:T(8,128)(2,1)}, u32[]{:S(2)}) copy-start(bf16[256,256]{1,0:T(8,128)(2,1)} %constant.16.clone.refs_9_.refs_12_.refs_15_) | copy-start | bytes 393220
  17.1 8.5 %collective-permute-start.8 = (bf16[2,560,128]{2,1,0:T(8,128)(2,1)S(1)}, bf16[2,560,128]{2,1,0:T(8,128)(2,1)S(1)}, u32[]{:S(2)}, u32[]{:S(2)}) collective-permute-start(bf16[2,560,128]{2,1,0:T(8,128)(2,1)S(1)} %constant_dynamic-update-slice_fusion), channel_id=1, source_target_pairs={{0,4},{4,0},{8,12},{12,8},{16,20},{20,16},{24,28},{28,24},{1,5},{5... | collective-permute-start | bytes 860168 | tf_op jit(solution)/shard_map/ppermute | solution.py:423
  18.5 8.5 %collective-permute-start.7 = (bf16[2,560,128]{2,1,0:T(8,128)(2,1)S(1)}, bf16[2,560,128]{2,1,0:T(8,128)(2,1)S(1)}, u32[]{:S(2)}, u32[]{:S(2)}) collective-permute-start(bf16[2,560,128]{2,1,0:T(8,128)(2,1)S(1)} %constant_dynamic-update-slice_fusion), channel_id=1, source_target_pairs={{0,2},{1,3},{2,0},{3,1},{4,6},{5,7},{6,4},{7,5},{8,10},{9,11},{10,... | collective-permute-start | bytes 860168 | tf_op jit(solution)/shard_map/ppermute | solution.py:423
  20.1 8.3 %collective-permute-start.9 = (bf16[2,560,128]{2,1,0:T(8,128)(2,1)S(1)}, bf16[2,560,128]{2,1,0:T(8,128)(2,1)S(1)}, u32[]{:S(2)}, u32[]{:S(2)}) collective-permute-start(bf16[2,560,128]{2,1,0:T(8,128)(2,1)S(1)} %pad_maximum_fusion), channel_id=1, source_target_pairs={{0,8},{4,12},{8,0},{12,4},{16,24},{20,28},{24,16},{28,20},{1,9},{5... | collective-permute-start | bytes 860168 | tf_op jit(solution)/shard_map/ppermute | solution.py:423
  28.4 7.3 %collective-permute-start.10 = (bf16[1,560,128]{2,1,0:T(8,128)(2,1)S(1)}, bf16[1,560,128]{2,1,0:T(8,128)(2,1)S(1)}, u32[]{:S(2)}, u32[]{:S(2)}) collective-permute-start(bf16[1,560,128]{2,1,0:T(8,128)(2,1)S(1)} %slice.10), channel_id=1, source_target_pairs={{0,4},{4,0},{8,12},{12,8},{16,20},{20,16},{24,28},{28,24},{1,5},{5... | collective-permute-start | bytes 430088 | tf_op jit(solution)/shard_map/ppermute | solution.py:423
  29.0 6.5 %collective-permute-start.12 = (bf16[1,560,128]{2,1,0:T(8,128)(2,1)S(1)}, bf16[1,560,128]{2,1,0:T(8,128)(2,1)S(1)}, u32[]{:S(2)}, u32[]{:S(2)}) collective-permute-start(bf16[1,560,128]{2,1,0:T(8,128)(2,1)S(1)} %slice.12), channel_id=1, source_target_pairs={{0,6},{1,7},{2,4},{3,5},{4,2},{5,3},{6,0},{7,1},{8,14},{9,15},{10,... | collective-permute-start | bytes 430088 | tf_op jit(solution)/shard_map/ppermute | solution.py:527
  30.5 6.7 %collective-permute-start.11 = (bf16[2,560,128]{2,1,0:T(8,128)(2,1)S(1)}, bf16[2,560,128]{2,1,0:T(8,128)(2,1)S(1)}, u32[]{:S(2)}, u32[]{:S(2)}) collective-permute-start(bf16[2,560,128]{2,1,0:T(8,128)(2,1)S(1)} %pad_maximum_fusion.1), channel_id=1, source_target_pairs={{0,8},{4,12},{8,0},{12,4},{16,24},{20,28},{24,16},{28,20},{1,9},{5... | collective-permute-start | bytes 860168 | tf_op jit(solution)/shard_map/ppermute | solution.py:423
  44.5 1.6 %collective-permute-start.13 = (f32[500,128]{1,0:T(8,128)S(1)}, f32[500,128]{1,0:T(8,128)S(1)}, u32[]{:S(2)}, u32[]{:S(2)}) collective-permute-start(f32[500,128]{1,0:T(8,128)S(1)} %get-tuple-element.42), channel_id=1, source_target_pairs={{0,1},{1,0},{2,3},{3,2},{4,5},{5,4},{6,7},{7,6},{8,9},{9,8},{10,11... | collective-permute-start | bytes 768008 | tf_op jit(solution)/shard_map/ppermute | solution.py:423
where the time goes:
time: 47.2 us; the launch traced here: 47 us
  starting transfers between devices  17 us (36%)
  Pallas kernels  15.5 us (33%)
  waiting for transfers between devices  11.9 us (25%)
  local copies, waits for them, and re-layouts  1.73 us (4%)
  between operations  0.85 us (2%)
    pallas_call x3, Pallas kernels, near_part(): pl.pallas_call(functools.partial(near_kernel, row_total, col_total, part)...  14 us
    ppermute x12, starting transfers between devices, swap(): return lax.ppermute(values, axis, [(i, i ^ flip) for i in range(size)])  13 us
    ppermute x12, waiting for transfers between devices, swap(): return lax.ppermute(values, axis, [(i, i ^ flip) for i in range(size)])  11.9 us
    ppermute x2, starting transfers between devices, corner_swap(): return lax.ppermute(values, ('row', 'col'), pairs)  4 us
    unnamed x19, local copies, waits for them, and re-layouts  1.67 us
    pallas_call x1, Pallas kernels, finish(): pl.pallas_call(finish_kernel, out_shape=jax.ShapeDtypeStruct((1, LIVE * G...  0.96 us
  transfers between devices with their start and end apart: 14, of which 8 were waited for; matrix products, arithmetic and copies ran while one was open for 0% of the time, Pallas kernels for 15%

commit v1 on v0

--- a/solution.py
+++ b/solution.py
@@ -23,7 +23,6 @@
 FLAT_ROWS = SIDE * CHUNK * 5 + 8
 DUO = 2 * GX
 QUAD = 4 * GX
-GROUP = 10
 VMEM_LIMIT = 20 * 1024 * 1024
 screen_width = 0.9
 F32 = jnp.float32
@@ -122,14 +121,6 @@
 
 def unfold(values):
     return jnp.concatenate([values[:, :LANES], values[:, LANES:]], axis=0)
-
-
-def in_groups(body):
-    def group(outer, carry):
-        body([outer * GROUP + inner for inner in range(GROUP)])
-        return carry
-
-    lax.fori_loop(0, GX // 4 // GROUP, group, 0)
 
 
 def quad(step):
@@ -241,11 +232,10 @@
             partner_ref[pl.ds(third * PACK, PACK), :] = wide[:, third * LANES : (third + 1) * LANES]
 
         def forward(steps):
-            values = []
-            for step in steps:
-                wave = jnp.where(is_mate, wave_refs[1][quad(step), :], wave_refs[0][quad(step), :])
-                values.append(partner_ref[quad(step), :] * wave)
-            values = [contract_lanes(v, z_ref[...]) for v in values]
+            planes = pl.ds(steps[0] * QUAD, len(steps) * QUAD)
+            wave = jnp.where(is_mate, wave_refs[1][planes, :], wave_refs[0][planes, :])
+            values = contract_lanes(partner_ref[planes, :] * wave, z_ref[...])
+            values = [values[i * QUAD : (i + 1) * QUAD] for i in range(len(steps))]
             values = [contract_rows(row_ref[...], fold(v)) for v in values]
             for step, v in zip(steps, values):
                 work_ref[quad(step), :] = unfold(v)
@@ -259,16 +249,16 @@
                 store_planes(work2_ref, step, v)
 
         def back(steps):
+            planes = pl.ds(steps[0] * QUAD, len(steps) * QUAD)
             values = [fold(work2_ref[quad(step), :]) for step in steps]
             values = [unfold(contract_rows(row_back_ref[...], v)) for v in values]
-            values = [contract_lanes(v, z_back_ref[...]) for v in values]
-            for step, v in zip(steps, values):
-                v = v * partner_ref[quad(step), :]
-                for sum_ref, scale in zip(sum_refs, scales):
-                    sum_ref[quad(step), :] = sum_ref[quad(step), :] + v * scale
+            values = contract_lanes(jnp.concatenate(values, axis=0), z_back_ref[...])
+            values = values * partner_ref[planes, :]
+            for sum_ref, scale in zip(sum_refs, scales):
+                sum_ref[planes, :] = sum_ref[planes, :] + values * scale
 
         for phase in (forward, across, back):
-            in_groups(phase)
+            phase(range(GX // 4))
         return carry
 
     lax.fori_loop(0, count, trio, 0)
@@ -528,24 +518,24 @@
 
     counts = list_counts(pair_list, pair_count)
     own = add_counts(pack_band(orbitals), col_total, counts, col_swap(counts, 1))
-    mate, x, y, z = col_swap(own, 1), col_swap(own, 2), row_swap(own, 1), row_swap(own, 2)
-    xy, w = corner_swap(own), row_swap(own, 4)
-    mate, x, y, z, xy, w = lax.optimization_barrier((mate, x, y, z, xy, w))
-    over_x, over_y, over_z = (
-        col_swap(both(w, z), 2),
-        row_swap(both(w, z), 1),
-        row_swap(both(w, xy), 2),
+    in_order = lambda *values: lax.optimization_barrier(values)
+    mate, x, y, xy, z, w = in_order(
+        col_swap(own, 1),
+        col_swap(own, 2),
+        row_swap(own, 1),
+        corner_swap(own),
+        row_swap(own, 2),
+        row_swap(own, 4),
     )
+    w_z, w_xy = in_order(both(w, z), both(w, xy))
+    over_x, over_y, over_z = col_swap(w_z, 2), row_swap(w_z, 1), row_swap(w_xy, 2)
     tables = [jnp.asarray(table) for table in solve_tables()]
     blocks = [own, w, z, y, x, xy]
     *waves, sum0, sum1 = near_part(row_total, col_total, 0, [*blocks, mate, *tables])
-    held = lax.optimization_barrier((sum0, sum1, over_x, over_y, over_z))
-    sum0, sum1, over_x, over_y, over_z = held
-    last = (
-        row_swap(over_x[:1], 1),
-        row_swap(both(over_x[:1], over_y[:1]), 2),
-        corner_swap(over_z[:1]),
-    )
+    sum0, sum1, over_x, over_y, over_z = in_order(sum0, sum1, over_x, over_y, over_z)
+    wx, wz, wx_wy = in_order(over_x[:1], over_z[:1], both(over_x[:1], over_y[:1]))
+    wxy, wzxy, over_z2 = in_order(row_swap(wx, 1), corner_swap(wz), row_swap(wx_wy, 2))
+    last = (wxy, over_z2, wzxy)
     for part, arrived in enumerate(((over_x, over_y, over_z), last), 1):
         blocks += arrived
         operands = [*blocks, mate, *tables, *waves, sum0, sum1]

time: 47.2 us -> 49.6 us (1.051); the launches traced: 47 us -> 50.5 us
  waiting for transfers between devices: 11.9 us -> 13.9 us
  local copies, waits for them, and re-layouts: 1.73 us -> 3.26 us
  Pallas kernels: 15.5 us -> 16.8 us
  starting transfers between devices: 17 us -> 15.7 us
    pallas_call x3, Pallas kernels: 14 us -> 15.3 us  [near_part(): pl.pallas_call(functools.partial(near_kernel, row_total, col_total, part)...]
    ppermute x12, starting transfers between devices: 13 us -> 11.7 us  [swap(): return lax.ppermute(values, axis, [(i, i ^ flip) for i in range(size)])]
    ppermute x12, waiting for transfers between devices: 11.9 us -> 13 us  [swap(): return lax.ppermute(values, axis, [(i, i ^ flip) for i in range(size)])]
    slice x1 -> x2, local copies, waits for them, and re-layouts: 0.01 us -> 0.89 us  [near_shards(): over_y[:1]]
    ppermute x2, waiting for transfers between devices: 0.01 us -> 0.85 us  [corner_swap(): return lax.ppermute(values, ('row', 'col'), pairs)]
    unnamed x19 -> x22, local copies, waits for them, and re-layouts: 1.67 us -> 2.35 us
  transfers between devices with their start and end apart: 14 -> 14, of which waited for: 8 -> 9; matrix products, arithmetic and copies ran while one was open for 0% -> 0% of each run, Pallas kernels for 15% -> 15%
where the time goes in v1:
time: 49.6 us; the launch traced here: 50.5 us
  Pallas kernels  16.8 us (34%)
  starting transfers between devices  15.7 us (32%)
  waiting for transfers between devices  13.9 us (28%)
  local copies, waits for them, and re-layouts  3.26 us (7%)
  between operations  0.83 us (2%)
    pallas_call x3, Pallas kernels, near_part(): pl.pallas_call(functools.partial(near_kernel, row_total, col_total, part)...  15.3 us
    ppermute x12, waiting for transfers between devices, swap(): return lax.ppermute(values, axis, [(i, i ^ flip) for i in range(size)])  13 us
    ppermute x12, starting transfers between devices, swap(): return lax.ppermute(values, axis, [(i, i ^ flip) for i in range(size)])  11.7 us
    ppermute x2, starting transfers between devices, corner_swap(): return lax.ppermute(values, ('row', 'col'), pairs)  3.94 us
    unnamed x22, local copies, waits for them, and re-layouts  2.35 us
  transfers between devices with their start and end apart: 14, of which 9 were waited for; matrix products, arithmetic and copies ran while one was open for 0% of the time, Pallas kernels for 15%

profile of v1, /device:TPU:0, one launch (start us, length us, event | category | flops | bytes accessed | tf_op | source)
XLA Modules:
  0.0 50.5 jit_solution(5706194955668404410)
XLA Ops:
  0.7 0.7 %copy-done.3 = s32[1,8,2]{1,2,0:T(2,128)S(1)} copy-done((s32[1,8,2]{1,2,0:T(2,128)S(1)}, s32[1,8,2]{1,2,0:T(2,128)}, u32[]{:S(2)}) %copy-start.3) | copy-done | bytes 88
  1.3 0.2 list_counts.1.own_ref
  1.5 0.5 collective-permute-start
  2.0 0.9 %copy-done = bf16[1,64000]{1,0:T(2,128)(2,1)S(1)} copy-done((bf16[1,64000]{1,0:T(2,128)(2,1)S(1)}, bf16[1,64000]{1,0:T(2,128)(2,1)}, u32[]{:S(2)}) %copy-start) | copy-done | bytes 128024
  2.9 0.4 pack_band.1.packed_ref
  3.4 3.7 %collective-permute-start.6 = (bf16[1,560,128]{2,1,0:T(8,128)(2,1)S(1)}, bf16[1,560,128]{2,1,0:T(8,128)(2,1)S(1)}, u32[]{:S(2)}, u32[]{:S(2)}) collective-permute-start(bf16[1,560,128]{2,1,0:T(8,128)(2,1)S(1)} %add_counts.1.refs_0_), channel_id=1, source_target_pairs={{0,16},{4,20},{8,24},{12,28},{16,0},{20,4},{24,8},{28,12},{1,17},{... | collective-permute-start | bytes 430088 | tf_op jit(solution)/shard_map/ppermute | solution.py:413
  7.1 1.6 %collective-permute-start.5 = (bf16[1,560,128]{2,1,0:T(8,128)(2,1)S(1)}, bf16[1,560,128]{2,1,0:T(8,128)(2,1)S(1)}, u32[]{:S(2)}, u32[]{:S(2)}) collective-permute-start(bf16[1,560,128]{2,1,0:T(8,128)(2,1)S(1)} %add_counts.1.refs_0_), channel_id=1, source_target_pairs={{0,8},{4,12},{8,0},{12,4},{16,24},{20,28},{24,16},{28,20},{1,9},{5... | collective-permute-start | bytes 430088 | tf_op jit(solution)/shard_map/ppermute | solution.py:413
  8.6 2.4 %collective-permute-start.4 = (bf16[1,560,128]{2,1,0:T(8,128)(2,1)S(1)}, bf16[1,560,128]{2,1,0:T(8,128)(2,1)S(1)}, u32[]{:S(2)}, u32[]{:S(2)}) collective-permute-start(bf16[1,560,128]{2,1,0:T(8,128)(2,1)S(1)} %add_counts.1.refs_0_), channel_id=1, source_target_pairs={{0,6},{1,7},{2,4},{3,5},{4,2},{5,3},{6,0},{7,1},{8,14},{9,15},{10,... | collective-permute-start | bytes 430088 | tf_op jit(solution)/shard_map/ppermute | solution.py:517
  11.1 0.5 %collective-permute-start.3 = (bf16[1,560,128]{2,1,0:T(8,128)(2,1)S(1)}, bf16[1,560,128]{2,1,0:T(8,128)(2,1)S(1)}, u32[]{:S(2)}, u32[]{:S(2)}) collective-permute-start(bf16[1,560,128]{2,1,0:T(8,128)(2,1)S(1)} %add_counts.1.refs_0_), channel_id=1, source_target_pairs={{0,4},{4,0},{8,12},{12,8},{16,20},{20,16},{24,28},{28,24},{1,5},{5... | collective-permute-start | bytes 430088 | tf_op jit(solution)/shard_map/ppermute | solution.py:413
  11.6 0.5 %collective-permute-start.2 = (bf16[1,560,128]{2,1,0:T(8,128)(2,1)S(1)}, bf16[1,560,128]{2,1,0:T(8,128)(2,1)S(1)}, u32[]{:S(2)}, u32[]{:S(2)}) collective-permute-start(bf16[1,560,128]{2,1,0:T(8,128)(2,1)S(1)} %add_counts.1.refs_0_), channel_id=1, source_target_pairs={{0,2},{1,3},{2,0},{3,1},{4,6},{5,7},{6,4},{7,5},{8,10},{9,11},{10,... | collective-permute-start | bytes 430088 | tf_op jit(solution)/shard_map/ppermute | solution.py:413
  12.1 2.5 %collective-permute-done.6.refs_1_ = bf16[1,560,128]{2,1,0:T(8,128)(2,1)S(1)} collective-permute-done((bf16[1,560,128]{2,1,0:T(8,128)(2,1)S(1)}, bf16[1,560,128]{2,1,0:T(8,128)(2,1)S(1)}, u32[]{:S(2)}, u32[]{:S(2)}) %collective-permute-start.6) | collective-permute-done | bytes 143392 | tf_op jit(solution)/shard_map/ppermute | solution.py:413
  14.7 0.2 collective-permute-done.5.refs_2_
  14.9 0.9 %collective-permute-done.4.refs_5_ = bf16[1,560,128]{2,1,0:T(8,128)(2,1)S(1)} collective-permute-done((bf16[1,560,128]{2,1,0:T(8,128)(2,1)S(1)}, bf16[1,560,128]{2,1,0:T(8,128)(2,1)S(1)}, u32[]{:S(2)}, u32[]{:S(2)}) %collective-permute-start.4) | collective-permute-done | bytes 143392 | tf_op jit(solution)/shard_map/ppermute | solution.py:517
  15.7 2.5 %collective-permute-done.3.refs_3_ = bf16[1,560,128]{2,1,0:T(8,128)(2,1)S(1)} collective-permute-done((bf16[1,560,128]{2,1,0:T(8,128)(2,1)S(1)}, bf16[1,560,128]{2,1,0:T(8,128)(2,1)S(1)}, u32[]{:S(2)}, u32[]{:S(2)}) %collective-permute-start.3) | collective-permute-done | bytes 143392 | tf_op jit(solution)/shard_map/ppermute | solution.py:413
  18.2 0.1 collective-permute-done.2.refs_4_
  18.4 1.5 %collective-permute-start.8 = (bf16[2,560,128]{2,1,0:T(8,128)(2,1)S(1)}, bf16[2,560,128]{2,1,0:T(8,128)(2,1)S(1)}, u32[]{:S(2)}, u32[]{:S(2)}) collective-permute-start(bf16[2,560,128]{2,1,0:T(8,128)(2,1)S(1)} %get-tuple-element.40), channel_id=1, source_target_pairs={{0,4},{4,0},{8,12},{12,8},{16,20},{20,16},{24,28},{28,24},{1,5},{5... | collective-permute-start | bytes 860168 | tf_op jit(solution)/shard_map/ppermute | solution.py:413
  19.9 0.8 %collective-permute-start.7 = (bf16[2,560,128]{2,1,0:T(8,128)(2,1)S(1)}, bf16[2,560,128]{2,1,0:T(8,128)(2,1)S(1)}, u32[]{:S(2)}, u32[]{:S(2)}) collective-permute-start(bf16[2,560,128]{2,1,0:T(8,128)(2,1)S(1)} %get-tuple-element.40), channel_id=1, source_target_pairs={{0,2},{1,3},{2,0},{3,1},{4,6},{5,7},{6,4},{7,5},{8,10},{9,11},{10,... | collective-permute-start | bytes 860168 | tf_op jit(solution)/shard_map/ppermute | solution.py:413
  20.7 0.4 collective-permute-start.9
  21.2 3.7 %solve_part.3 = (f32[1680,128]{1,0:T(8,128)S(1)}, f32[1680,128]{1,0:T(8,128)S(1)}, f32[1680,128]{1,0:T(8,128)S(1)}, f32[1680,128]{1,0:T(8,128)S(1)}) custom-call(bf16[1,560,128]{2,1,0:T(8,128)(2,1)S(1)} %add_counts.1.refs_0_, bf16[1,560,128]{2,1,0:T(8,128)(2,1)S(1)} %collective-permute-done.6.refs_1_, ...), custom_call_target="tpu_custom_call" | custom-call | flops 4000000000 | bytes 20000000 | tf_op jit(solution)/shard_map/solve_part/pallas_call | solution.py:487
  24.9 3.5 %collective-permute-done.9.refs_8_ = bf16[2,560,128]{2,1,0:T(8,128)(2,1)S(1)} collective-permute-done((bf16[2,560,128]{2,1,0:T(8,128)(2,1)S(1)}, bf16[2,560,128]{2,1,0:T(8,128)(2,1)S(1)}, u32[]{:S(2)}, u32[]{:S(2)}) %collective-permute-start.9) | collective-permute-done | bytes 286752 | tf_op jit(solution)/shard_map/ppermute | solution.py:413
  28.4 0.7 %copy-done.1 = bf16[2,560,128]{2,1,0:T(8,128)(2,1)} copy-done((bf16[2,560,128]{2,1,0:T(8,128)(2,1)}, bf16[2,560,128]{2,1,0:T(8,128)(2,1)S(1)}, u32[]{:S(2)}) %copy-start.1) | copy-done | bytes 286744
  29.1 0.9 %slice-done = bf16[1,560,128]{2,1,0:T(8,128)(2,1)S(1)} async-done(((bf16[2,560,128]{2,1,0:T(8,128)(2,1)}), bf16[1,560,128]{2,1,0:T(8,128)(2,1)S(1)}, s32[]{:S(2)}) %slice-start) | async-done | bytes 143384 | tf_op jit(solution)/shard_map/slice | solution.py:536
  30.0 1.7 %collective-permute-start.10 = (bf16[1,560,128]{2,1,0:T(8,128)(2,1)S(1)}, bf16[1,560,128]{2,1,0:T(8,128)(2,1)S(1)}, u32[]{:S(2)}, u32[]{:S(2)}) collective-permute-start(bf16[1,560,128]{2,1,0:T(8,128)(2,1)S(1)} %slice.10), channel_id=1, source_target_pairs={{0,4},{4,0},{8,12},{12,8},{16,20},{20,16},{24,28},{28,24},{1,5},{5... | collective-permute-start | bytes 430088 | tf_op jit(solution)/shard_map/ppermute | solution.py:413
  31.8 1.5 %collective-permute-start.11 = (bf16[1,560,128]{2,1,0:T(8,128)(2,1)S(1)}, bf16[1,560,128]{2,1,0:T(8,128)(2,1)S(1)}, u32[]{:S(2)}, u32[]{:S(2)}) collective-permute-start(bf16[1,560,128]{2,1,0:T(8,128)(2,1)S(1)} %slice.11), channel_id=1, source_target_pairs={{0,6},{1,7},{2,4},{3,5},{4,2},{5,3},{6,0},{7,1},{8,14},{9,15},{10,... | collective-permute-start | bytes 430088 | tf_op jit(solution)/shard_map/ppermute | solution.py:517
  33.3 0.4 collective-permute-start.12
  33.7 3.6 %solve_part.4 = (f32[1680,128]{1,0:T(8,128)S(1)}, f32[1680,128]{1,0:T(8,128)S(1)}) custom-call(bf16[1,560,128]{2,1,0:T(8,128)(2,1)S(1)} %add_counts.1.refs_0_, bf16[1,560,128]{2,1,0:T(8,128)(2,1)S(1)} %collective-permute-done.6.refs_1_, bf16[1,560,128]{2,1,0:T(8,128)(2,1)S(1)} %collective-permute-done.5.refs_2_, ...), custom_call_target="tpu_custom_call" | custom-call | flops 4000000000 | bytes 20000000 | tf_op jit(solution)/shard_map/solve_part/pallas_call | solution.py:487
  37.3 0.7 %collective-permute-done.10.refs_9_ = bf16[1,560,128]{2,1,0:T(8,128)(2,1)S(1)} collective-permute-done((bf16[1,560,128]{2,1,0:T(8,128)(2,1)S(1)}, bf16[1,560,128]{2,1,0:T(8,128)(2,1)S(1)}, u32[]{:S(2)}, u32[]{:S(2)}) %collective-permute-start.10) | collective-permute-done | bytes 143392 | tf_op jit(solution)/shard_map/ppermute | solution.py:413
  38.0 1.9 %collective-permute-done.12.refs_10_ = bf16[2,560,128]{2,1,0:T(8,128)(2,1)S(1)} collective-permute-done((bf16[2,560,128]{2,1,0:T(8,128)(2,1)S(1)}, bf16[2,560,128]{2,1,0:T(8,128)(2,1)S(1)}, u32[]{:S(2)}, u32[]{:S(2)}) %collective-permute-start.12) | collective-permute-done | bytes 286752 | tf_op jit(solution)/shard_map/ppermute | solution.py:413
  40.0 8.0 %solve_part.5 = (f32[500,128]{1,0:T(8,128)S(1)}, f32[500,128]{1,0:T(8,128)S(1)}) custom-call(bf16[1,560,128]{2,1,0:T(8,128)(2,1)S(1)} %add_counts.1.refs_0_, bf16[1,560,128]{2,1,0:T(8,128)(2,1)S(1)} %collective-permute-done.6.refs_1_, bf16[1,560,128]{2,1,0:T(8,128)(2,1)S(1)} %collective-permute-done.5.refs_2_, ...), custom_call_target="tpu_custom_call" | custom-call | flops 4000000000 | bytes 20000000 | tf_op jit(solution)/shard_map/solve_part/pallas_call | solution.py:487
  48.0 0.1 collective-permute-start.13
  48.1 1.5 %collective-permute-done.13.part_ref = f32[500,128]{1,0:T(8,128)S(1)} collective-permute-done((f32[500,128]{1,0:T(8,128)S(1)}, f32[500,128]{1,0:T(8,128)S(1)}, u32[]{:S(2)}, u32[]{:S(2)}) %collective-permute-start.13) | collective-permute-done | bytes 256032 | tf_op jit(solution)/shard_map/ppermute | solution.py:413
  49.6 1.0 %add_parts.1 = f32[1,64000]{1,0:T(1,128)} custom-call(f32[500,128]{1,0:T(8,128)S(1)} %get-tuple-element.57.own_ref, f32[500,128]{1,0:T(8,128)S(1)} %collective-permute-done.13.part_ref), custom_call_target="tpu_custom_call" | custom-call | tf_op jit(solution)/shard_map/add_parts/pallas_call | solution.py:459
  (31 shorter events, 0.2 us)
Async XLA Ops:
  0.7 0.7 %copy-start.3 = (s32[1,8,2]{1,2,0:T(2,128)S(1)}, s32[1,8,2]{1,2,0:T(2,128)}, u32[]{:S(2)}) copy-start(s32[1,8,2]{1,2,0:T(2,128)} %param.11) | copy-start | bytes 196
  1.5 1.8 %collective-permute-start = (f32[16,128]{1,0:T(8,128)S(1)}, f32[16,128]{1,0:T(8,128)S(1)}, u32[]{:S(2)}, u32[]{:S(2)}) collective-permute-start(f32[16,128]{1,0:T(8,128)S(1)} %list_counts.1.own_ref), channel_id=1, source_target_pairs={{0,1},{1,0},{2,3},{3,2},{4,5},{5,4},{6,7},{7,6},{8,9},{9,8},{10,11... | collective-permute-start | bytes 24584 | tf_op jit(solution)/shard_map/ppermute | solution.py:413
  2.0 0.9 %copy-start = (bf16[1,64000]{1,0:T(2,128)(2,1)S(1)}, bf16[1,64000]{1,0:T(2,128)(2,1)}, u32[]{:S(2)}) copy-start(bf16[1,64000]{1,0:T(2,128)(2,1)} %band_ref.1) | copy-start | bytes 384004
  2.9 18.2 %copy-start.4 = (f32[1600,128]{1,0:T(8,128)S(1)}, f32[1600,128]{1,0:T(8,128)}, u32[]{:S(2)}) copy-start(f32[1600,128]{1,0:T(8,128)} %constant.20.clone.refs_13_.refs_16_.refs_19_) | copy-start | bytes 2457604
  3.3 17.8 %copy-start.5 = (bf16[384,384]{1,0:T(8,128)(2,1)S(1)}, bf16[384,384]{1,0:T(8,128)(2,1)}, u32[]{:S(2)}) copy-start(bf16[384,384]{1,0:T(8,128)(2,1)} %constant.14.clone.refs_7_.refs_10_.refs_13_) | copy-start | bytes 884740
  3.3 17.8 %copy-start.6 = (bf16[256,256]{1,0:T(8,128)(2,1)S(1)}, bf16[256,256]{1,0:T(8,128)(2,1)}, u32[]{:S(2)}) copy-start(bf16[256,256]{1,0:T(8,128)(2,1)} %constant.17.clone.refs_10_.refs_13_.refs_16_) | copy-start | bytes 393220
  3.3 17.8 %copy-start.7 = (bf16[256,256]{1,0:T(8,128)(2,1)S(1)}, bf16[256,256]{1,0:T(8,128)(2,1)}, u32[]{:S(2)}) copy-start(bf16[256,256]{1,0:T(8,128)(2,1)} %constant.16.clone.refs_9_.refs_12_.refs_15_) | copy-start | bytes 393220
  3.4 17.8 %copy-start.8 = (bf16[128,384]{1,0:T(8,128)(2,1)S(1)}, bf16[128,384]{1,0:T(8,128)(2,1)}, u32[]{:S(2)}) copy-start(bf16[128,384]{1,0:T(8,128)(2,1)} %constant.15.clone.refs_8_.refs_11_.refs_14_) | copy-start | bytes 294916
  3.4 17.8 %copy-start.9 = (bf16[80,240]{1,0:T(8,128)(2,1)S(1)}, bf16[80,240]{1,0:T(8,128)(2,1)}, u32[]{:S(2)}) copy-start(bf16[80,240]{1,0:T(8,128)(2,1)} %constant.19.clone.refs_12_.refs_15_.refs_18_) | copy-start | bytes 115204
  3.4 17.8 %copy-start.10 = (bf16[80,240]{1,0:T(8,128)(2,1)S(1)}, bf16[80,240]{1,0:T(8,128)(2,1)}, u32[]{:S(2)}) copy-start(bf16[80,240]{1,0:T(8,128)(2,1)} %constant.18.clone.refs_11_.refs_14_.refs_17_) | copy-start | bytes 115204
  3.4 11.3 %collective-permute-start.6 = (bf16[1,560,128]{2,1,0:T(8,128)(2,1)S(1)}, bf16[1,560,128]{2,1,0:T(8,128)(2,1)S(1)}, u32[]{:S(2)}, u32[]{:S(2)}) collective-permute-start(bf16[1,560,128]{2,1,0:T(8,128)(2,1)S(1)} %add_counts.1.refs_0_), channel_id=1, source_target_pairs={{0,16},{4,20},{8,24},{12,28},{16,0},{20,4},{24,8},{28,12},{1,17},{... | collective-permute-start | bytes 430088 | tf_op jit(solution)/shard_map/ppermute | solution.py:413
  7.1 7.8 %collective-permute-start.5 = (bf16[1,560,128]{2,1,0:T(8,128)(2,1)S(1)}, bf16[1,560,128]{2,1,0:T(8,128)(2,1)S(1)}, u32[]{:S(2)}, u32[]{:S(2)}) collective-permute-start(bf16[1,560,128]{2,1,0:T(8,128)(2,1)S(1)} %add_counts.1.refs_0_), channel_id=1, source_target_pairs={{0,8},{4,12},{8,0},{12,4},{16,24},{20,28},{24,16},{28,20},{1,9},{5... | collective-permute-start | bytes 430088 | tf_op jit(solution)/shard_map/ppermute | solution.py:413
  8.6 7.1 %collective-permute-start.4 = (bf16[1,560,128]{2,1,0:T(8,128)(2,1)S(1)}, bf16[1,560,128]{2,1,0:T(8,128)(2,1)S(1)}, u32[]{:S(2)}, u32[]{:S(2)}) collective-permute-start(bf16[1,560,128]{2,1,0:T(8,128)(2,1)S(1)} %add_counts.1.refs_0_), channel_id=1, source_target_pairs={{0,6},{1,7},{2,4},{3,5},{4,2},{5,3},{6,0},{7,1},{8,14},{9,15},{10,... | collective-permute-start | bytes 430088 | tf_op jit(solution)/shard_map/ppermute | solution.py:517
  11.1 7.1 %collective-permute-start.3 = (bf16[1,560,128]{2,1,0:T(8,128)(2,1)S(1)}, bf16[1,560,128]{2,1,0:T(8,128)(2,1)S(1)}, u32[]{:S(2)}, u32[]{:S(2)}) collective-permute-start(bf16[1,560,128]{2,1,0:T(8,128)(2,1)S(1)} %add_counts.1.refs_0_), channel_id=1, source_target_pairs={{0,4},{4,0},{8,12},{12,8},{16,20},{20,16},{24,28},{28,24},{1,5},{5... | collective-permute-start | bytes 430088 | tf_op jit(solution)/shard_map/ppermute | solution.py:413
  11.6 6.7 %collective-permute-start.2 = (bf16[1,560,128]{2,1,0:T(8,128)(2,1)S(1)}, bf16[1,560,128]{2,1,0:T(8,128)(2,1)S(1)}, u32[]{:S(2)}, u32[]{:S(2)}) collective-permute-start(bf16[1,560,128]{2,1,0:T(8,128)(2,1)S(1)} %add_counts.1.refs_0_), channel_id=1, source_target_pairs={{0,2},{1,3},{2,0},{3,1},{4,6},{5,7},{6,4},{7,5},{8,10},{9,11},{10,... | collective-permute-start | bytes 430088 | tf_op jit(solution)/shard_map/ppermute | solution.py:413
  14.7 3.6 %collective-permute-start.1 = (bf16[1,560,128]{2,1,0:T(8,128)(2,1)S(1)}, bf16[1,560,128]{2,1,0:T(8,128)(2,1)S(1)}, u32[]{:S(2)}, u32[]{:S(2)}) collective-permute-start(bf16[1,560,128]{2,1,0:T(8,128)(2,1)S(1)} %add_counts.1.refs_0_), channel_id=1, source_target_pairs={{0,1},{1,0},{2,3},{3,2},{4,5},{5,4},{6,7},{7,6},{8,9},{9,8},{10,11... | collective-permute-start | bytes 430088 | tf_op jit(solution)/shard_map/ppermute | solution.py:413
  18.4 10.0 %collective-permute-start.8 = (bf16[2,560,128]{2,1,0:T(8,128)(2,1)S(1)}, bf16[2,560,128]{2,1,0:T(8,128)(2,1)S(1)}, u32[]{:S(2)}, u32[]{:S(2)}) collective-permute-start(bf16[2,560,128]{2,1,0:T(8,128)(2,1)S(1)} %get-tuple-element.40), channel_id=1, source_target_pairs={{0,4},{4,0},{8,12},{12,8},{16,20},{20,16},{24,28},{28,24},{1,5},{5... | collective-permute-start | bytes 860168 | tf_op jit(solution)/shard_map/ppermute | solution.py:413
  19.9 8.5 %collective-permute-start.7 = (bf16[2,560,128]{2,1,0:T(8,128)(2,1)S(1)}, bf16[2,560,128]{2,1,0:T(8,128)(2,1)S(1)}, u32[]{:S(2)}, u32[]{:S(2)}) collective-permute-start(bf16[2,560,128]{2,1,0:T(8,128)(2,1)S(1)} %get-tuple-element.40), channel_id=1, source_target_pairs={{0,2},{1,3},{2,0},{3,1},{4,6},{5,7},{6,4},{7,5},{8,10},{9,11},{10,... | collective-permute-start | bytes 860168 | tf_op jit(solution)/shard_map/ppermute | solution.py:413
  20.7 7.7 %collective-permute-start.9 = (bf16[2,560,128]{2,1,0:T(8,128)(2,1)S(1)}, bf16[2,560,128]{2,1,0:T(8,128)(2,1)S(1)}, u32[]{:S(2)}, u32[]{:S(2)}) collective-permute-start(bf16[2,560,128]{2,1,0:T(8,128)(2,1)S(1)} %get-tuple-element.41), channel_id=1, source_target_pairs={{0,8},{4,12},{8,0},{12,4},{16,24},{20,28},{24,16},{28,20},{1,9},{5... | collective-permute-start | bytes 860168 | tf_op jit(solution)/shard_map/ppermute | solution.py:413
  28.4 0.7 %copy-start.1 = (bf16[2,560,128]{2,1,0:T(8,128)(2,1)}, bf16[2,560,128]{2,1,0:T(8,128)(2,1)S(1)}, u32[]{:S(2)}) copy-start(bf16[2,560,128]{2,1,0:T(8,128)(2,1)S(1)} %collective-permute-done.8.refs_7_) | copy-start | bytes 860164
  29.1 0.9 %slice-start = ((bf16[2,560,128]{2,1,0:T(8,128)(2,1)}), bf16[1,560,128]{2,1,0:T(8,128)(2,1)S(1)}, s32[]{:S(2)}) async-start(bf16[2,560,128]{2,1,0:T(8,128)(2,1)} %copy-done.1), calls=%async_computation | async-start | bytes 286720 | tf_op jit(solution)/shard_map/slice | solution.py:536
  30.0 3.7 %copy-start.2 = (bf16[2,560,128]{2,1,0:T(8,128)(2,1)S(1)}, bf16[2,560,128]{2,1,0:T(8,128)(2,1)}, u32[]{:S(2)}) copy-start(bf16[2,560,128]{2,1,0:T(8,128)(2,1)} %copy-done.1) | copy-start | bytes 860164
  30.0 8.0 %collective-permute-start.10 = (bf16[1,560,128]{2,1,0:T(8,128)(2,1)S(1)}, bf16[1,560,128]{2,1,0:T(8,128)(2,1)S(1)}, u32[]{:S(2)}, u32[]{:S(2)}) collective-permute-start(bf16[1,560,128]{2,1,0:T(8,128)(2,1)S(1)} %slice.10), channel_id=1, source_target_pairs={{0,4},{4,0},{8,12},{12,8},{16,20},{20,16},{24,28},{28,24},{1,5},{5... | collective-permute-start | bytes 430088 | tf_op jit(solution)/shard_map/ppermute | solution.py:413
  31.8 6.3 %collective-permute-start.11 = (bf16[1,560,128]{2,1,0:T(8,128)(2,1)S(1)}, bf16[1,560,128]{2,1,0:T(8,128)(2,1)S(1)}, u32[]{:S(2)}, u32[]{:S(2)}) collective-permute-start(bf16[1,560,128]{2,1,0:T(8,128)(2,1)S(1)} %slice.11), channel_id=1, source_target_pairs={{0,6},{1,7},{2,4},{3,5},{4,2},{5,3},{6,0},{7,1},{8,14},{9,15},{10,... | collective-permute-start | bytes 430088 | tf_op jit(solution)/shard_map/ppermute | solution.py:517
  33.3 6.7 %collective-permute-start.12 = (bf16[2,560,128]{2,1,0:T(8,128)(2,1)S(1)}, bf16[2,560,128]{2,1,0:T(8,128)(2,1)S(1)}, u32[]{:S(2)}, u32[]{:S(2)}) collective-permute-start(bf16[2,560,128]{2,1,0:T(8,128)(2,1)S(1)} %pad_maximum_fusion.2), channel_id=1, source_target_pairs={{0,8},{4,12},{8,0},{12,4},{16,24},{20,28},{24,16},{28,20},{1,9},{5... | collective-permute-start | bytes 860168 | tf_op jit(solution)/shard_map/ppermute | solution.py:413
  48.0 1.6 %collective-permute-start.13 = (f32[500,128]{1,0:T(8,128)S(1)}, f32[500,128]{1,0:T(8,128)S(1)}, u32[]{:S(2)}, u32[]{:S(2)}) collective-permute-start(f32[500,128]{1,0:T(8,128)S(1)} %get-tuple-element.58), channel_id=1, source_target_pairs={{0,1},{1,0},{2,3},{3,2},{4,5},{5,4},{6,7},{7,6},{8,9},{9,8},{10,11... | collective-permute-start | bytes 768008 | tf_op jit(solution)/shard_map/ppermute | solution.py:413
